TPU v7x, 32 devices: a whole 2x2x4 slice. The times are simulated.
32 devices in a mesh: blk: 8 (over y, x, core), head: 4 (over z).
Axes of the slice: x: 2, y: 2, z: 4, core: 2. Of those that a mesh axis runs over, the one named last changes fastest.
Arguments:
- queries: bfloat16 [4096, 8192], P('blk', 'head'), may hold values from -120 to 120
- keys: bfloat16 [4096, 1024], P('blk', 'head'), may hold values from -6.5 to 6.5
- values: bfloat16 [4096, 1024], P('blk', 'head'), may hold values from -6 to 6
- w_out: bfloat16 [8192, 8192], P('head'), may hold values from -0.09375 to 0.09375
- order: int32 [16], replicated, may hold values from 0 to 15, each once
Outputs:
- mixed: bfloat16 [4096, 8192], P('blk', 'head')
Inputs may be any that keep to these rules, and one draw needn't show every extreme that they name: `order`: A permutation of 0 to 15.
All inputs are finite; a program needn't handle non-finite values.
Results may differ from a plain program's by a relative error of at most 0.015.
Values may be sent and summed in bfloat16 or wider, within the bound.
No kernel may reach another device: no remote copies, remote signals or barrier semaphores. Data moves between devices by JAX's collectives and lax.ppermute only.
A program may use at most 128 MiB of HBM per device.

v0:
```python
import functools
import math

import jax
import jax.numpy as jnp
from jax import lax
from jax.experimental import pallas as pl
from jax.experimental.pallas import tpu as pltpu
from jax.sharding import PartitionSpec as P

HD = 128
NT = (((1,), (1,)), ((), ()))
MIB = 2 ** 20
STEP = 4


def in_hbm(array):
    return pltpu.with_memory_space_constraint(array, pltpu.HBM)


def block_place(chunk, order_ref, me_ref):
    own = 2 * me_ref[0]
    return jnp.where(order_ref[own] > order_ref[own + 1], 1 - chunk, chunk)


def attend_kernel(half, tile, chunk, pieces, waited, order_ref, me_ref, q_ref, *refs):
    k_refs, v_refs = refs[:pieces], refs[pieces:2 * pieces]
    o_ref, inv, q_rows, k_all, v_wide, acc, top = refs[2 * pieces + waited:]
    blocks = order_ref.shape[0]
    per = blocks // pieces
    tok = q_ref.shape[0]
    group = q_ref.shape[1] // HD
    rows = group * tok
    shard = per * half
    factor = HD ** (-0.5) * math.log2(math.e)
    own = block_place(chunk, order_ref, me_ref)
    me = me_ref[0]

    def invert(b, _):
        inv[order_ref[b]] = jnp.bitwise_xor(b // per, me) * per + lax.rem(b, per)
        return 0

    lax.fori_loop(0, blocks, invert, 0)
    for g in range(group):
        q_rows[g * tok:(g + 1) * tok, :] = q_ref[:, g * HD:(g + 1) * HD]
    for r in range(pieces):
        k_all[r * shard:(r + 1) * shard, :] = k_refs[r][...]
        v_wide[r * shard:(r + 1) * shard, :HD] = v_refs[r][...]
    v_wide[:, HD:] = jnp.ones((v_wide.shape[0], HD), v_wide.dtype)
    earlier = order_ref[me * per + own]

    def block_of(ref, b):
        return ref[pl.ds(pl.multiple_of(b * half, half), half), :]

    def first(blocks_in):
        k_cat = jnp.concatenate([block_of(k_all, b) for b in blocks_in], axis=0)
        v_cat = jnp.concatenate([block_of(v_wide, b) for b in blocks_in], axis=0)
        width = k_cat.shape[0]
        query = lax.rem(lax.broadcasted_iota(jnp.int32, (tile, width), 0), tok)
        key = lax.broadcasted_iota(jnp.int32, (tile, width), 1) - (width - half)
        seen = key <= query
        for r in range(0, rows, tile):
            score = lax.dot_general(q_rows[r:r + tile, :], k_cat, NT,
                                    preferred_element_type=jnp.float32)
            score = jnp.where(seen, score, -1e30)
            peak = jnp.max(score, axis=1, keepdims=True)
            weight = jnp.exp2((score - peak) * factor)
            top[r:r + tile, :] = jnp.broadcast_to(peak, (tile, HD))
            acc[r:r + tile, :] = jnp.dot(weight.astype(jnp.bfloat16), v_cat,
                                         preferred_element_type=jnp.float32)

    def keys_of(blocks_in):
        return (jnp.concatenate([block_of(k_all, b) for b in blocks_in], axis=0),
                jnp.concatenate([block_of(v_wide, b) for b in blocks_in], axis=0))

    def over_tiles(k_cat, use):
        def scores(r):
            return lax.dot_general(q_rows[r:r + tile, :], k_cat, NT,
                                   preferred_element_type=jnp.float32)

        score = scores(0)
        for r in range(0, rows, tile):
            ahead = scores(r + tile) if r + tile < rows else None
            use(r, score)
            score = ahead

    def first(rest):
        k_cat, v_cat = keys_of([inv[earlier - rest + i] for i in range(rest)] + [own])
        query = lax.rem(lax.broadcasted_iota(jnp.int32, (tile, half), 0), tok)
        seen = lax.broadcasted_iota(jnp.int32, (tile, half), 1) <= query

        def use(r, score):
            masked = jnp.where(seen, score[:, rest * half:], -1e30)
            score = jnp.concatenate([score[:, :rest * half], masked], axis=1) if rest else masked
            peak = jnp.max(score, axis=1, keepdims=True)
            weight = jnp.exp2((score - peak) * factor)
            top[r:r + tile, :] = jnp.broadcast_to(peak, (tile, HD))
            acc[r:r + tile, :] = jnp.dot(weight.astype(jnp.bfloat16), v_cat,
                                         preferred_element_type=jnp.float32)

        over_tiles(k_cat, use)

    for rest in range(STEP):
        pl.when(lax.rem(earlier, STEP) == rest)(functools.partial(first, rest))

    def step(n, _):
        k_cat, v_cat = keys_of([inv[STEP * n + i] for i in range(STEP)])

        def use(r, score):
            old = top[r:r + tile, :]
            peak = jnp.maximum(old, jnp.max(score, axis=1, keepdims=True))
            top[r:r + tile, :] = peak
            wide = jnp.concatenate([peak] * (STEP * half // HD), axis=1)
            weight = jnp.exp2((score - wide) * factor)
            shrink = jnp.exp2((old - peak) * factor)
            acc[r:r + tile, :] = acc[r:r + tile, :] * jnp.concatenate(
                [shrink, shrink], axis=1) + jnp.dot(
                    weight.astype(jnp.bfloat16), v_cat, preferred_element_type=jnp.float32)

        over_tiles(k_cat, use)
        return 0

    lax.fori_loop(0, earlier // STEP, step, 0)
    for g in range(group):
        part = acc[g * tok:(g + 1) * tok, :]
        o_ref[:, g * HD:(g + 1) * HD] = (part[:, :HD] / part[:, HD:]).astype(o_ref.dtype)


def attend(queries, k_pieces, v_pieces, order, me, chunk, half, after=()):
    tok = half
    pieces = len(k_pieces)
    shard, kv_width = k_pieces[0].shape
    kv_local = kv_width // HD
    width = queries.shape[1] // kv_local
    keys = shard * pieces
    rows = width // HD * tok
    tile = min(rows, 256)
    piece_spec = pl.BlockSpec((shard, HD), lambda h, *_: (0, h))
    return pl.pallas_call(
        functools.partial(attend_kernel, half, tile, chunk, pieces, len(after)),
        out_shape=jax.ShapeDtypeStruct((tok, queries.shape[1]), jnp.bfloat16),
        grid_spec=pltpu.PrefetchScalarGridSpec(
            num_scalar_prefetch=2,
            grid=(kv_local,),
            in_specs=[pl.BlockSpec((tok, width), lambda h, *refs: (block_place(chunk, *refs), h))]
            + [piece_spec] * (2 * pieces)
            + [pl.BlockSpec(memory_space=pl.ANY)] * len(after),
            out_specs=pl.BlockSpec((tok, width), lambda h, *_: (0, h)),
            scratch_shapes=[
                pltpu.SMEM((order.shape[0],), jnp.int32),
                pltpu.VMEM((rows, HD), jnp.bfloat16),
                pltpu.VMEM((keys, HD), jnp.bfloat16),
                pltpu.VMEM((keys, 2 * HD), jnp.bfloat16),
                pltpu.VMEM((rows, 2 * HD), jnp.float32),
                pltpu.VMEM((rows, HD), jnp.float32),
            ],
        ),
        compiler_params=pltpu.CompilerParams(vmem_limit_bytes=40 * MIB),
        cost_estimate=pl.CostEstimate(flops=1, bytes_accessed=0, transcendentals=0),
        name="attend",
    )(order, me, in_hbm(queries), in_hbm(k_pieces[0]), *k_pieces[1:], in_hbm(v_pieces[0]), *v_pieces[1:], *after)


def exchange(arrays, axis, bits):
    count = lax.axis_size(axis)
    held = {0: arrays}
    for bit in bits:
        pairs = [(i, i ^ (1 << bit)) for i in range(count)]
        held.update({r ^ (1 << bit): lax.ppermute(a, axis, pairs) for r, a in held.items()})
    return [held[r] for r in range(count)]


def pick(z, options):
    value = jnp.int32(options[-1])
    for i in range(len(options) - 1):
        value = jnp.where(z == i, jnp.int32(options[i]), value)
    return value


def share_kernel(extra, blocks, z_ref, a_ref, w_ref, *refs):
    @pl.when(pick(z_ref[0], blocks) >= 0)
    def _():
        total = jnp.dot(a_ref[...], w_ref[...], preferred_element_type=jnp.float32)
        for ref in refs[:extra]:
            total = total + ref[...].astype(jnp.float32)
        refs[-1][...] = total.astype(refs[-1].dtype)


def share(attended, w_out, arrived, z, blocks, columns, after=(), kind=jnp.bfloat16):
    tok, depth = attended.shape
    wide = min(columns, 512)
    tiles = columns // wide
    extra = len(arrived)

    def at(j, z_ref):
        block = pick(z_ref[0], blocks)
        return (0, jnp.maximum(block, 0) * tiles + jnp.where(block >= 0, j, 0))

    def inside(j, z_ref):
        return (0, jnp.where(pick(z_ref[0], blocks) >= 0, j, 0))

    return pl.pallas_call(
        functools.partial(share_kernel, extra, blocks),
        out_shape=jax.ShapeDtypeStruct((tok, columns), kind),
        grid_spec=pltpu.PrefetchScalarGridSpec(
            num_scalar_prefetch=1,
            grid=(tiles,),
            in_specs=[
                pl.BlockSpec((tok, depth), lambda j, z_ref: (0, 0)),
                pl.BlockSpec((depth, wide), at),
            ] + [pl.BlockSpec((tok, wide), inside)] * extra
            + [pl.BlockSpec(memory_space=pl.ANY)] * len(after),
            out_specs=pl.BlockSpec((tok, wide), inside),
        ),
        compiler_params=pltpu.CompilerParams(vmem_limit_bytes=40 * MIB),
        cost_estimate=pl.CostEstimate(flops=1, bytes_accessed=0, transcendentals=0),
        name="share",
    )(z, attended, in_hbm(w_out), *arrived, *after)


def finish_kernel(extra, order_ref, me_ref, *refs):
    total = refs[0][...].astype(jnp.float32)
    for ref in refs[1:extra]:
        total = total + ref[...].astype(jnp.float32)
    refs[-1][...] = total.astype(jnp.bfloat16)


def finish(terms, order, me, chunk, whole_tok, out):
    tok, columns = terms[0].shape
    wide = min(columns, 1024)
    operands = list(terms)
    specs = [pl.BlockSpec((tok, wide), lambda j, *_: (0, j))] * len(terms)
    aliases = {}
    if out is not None:
        operands.append(out)
        specs.append(pl.BlockSpec(memory_space=pl.ANY))
        aliases = {1 + len(operands): 0}
    return pl.pallas_call(
        functools.partial(finish_kernel, len(terms)),
        out_shape=jax.ShapeDtypeStruct((whole_tok, columns), jnp.bfloat16),
        grid_spec=pltpu.PrefetchScalarGridSpec(
            num_scalar_prefetch=2,
            grid=(columns // wide,),
            in_specs=specs,
            out_specs=pl.BlockSpec((tok, wide), lambda j, *refs: (block_place(chunk, *refs), j)),
        ),
        input_output_aliases=aliases,
        compiler_params=pltpu.CompilerParams(vmem_limit_bytes=40 * MIB),
        cost_estimate=pl.CostEstimate(flops=1, bytes_accessed=0, transcendentals=0),
        name="finish",
    )(order, me, *operands)


def swap(array, pairs):
    return lax.ppermute(array, "head", pairs)


def line_of_four(attended, w_out, z, order, me, columns, tok):
    outer, inner, back = [(0, 1), (3, 2)], [(1, 2), (2, 1)], [(1, 0), (2, 3)]

    def part(a, arrived, blocks, after=(), kind=jnp.bfloat16):
        return share(a, w_out, arrived, z, blocks, columns, after, kind)

    far_end, near_end, last_end = (3, -1, -1, 0), (2, -1, -1, 1), (1, -1, -1, 2)
    far_on, near_on, home_on, all_own = (-1, 3, 0, -1), (-1, 2, 1, -1), (-1, 0, 3, -1), (0, 1, 2, 3)
    a0 = attended(0, [])
    far0 = part(a0, [], far_end)
    near0 = part(a0, [], near_end, [far0])
    a1 = attended(1, [near0])
    far0, near0 = swap(far0, outer), swap(near0, outer)
    far1 = part(a1, [], far_end)
    mid0 = part(a0, [far0], far_on, [far1])
    near1 = part(a1, [], near_end, [mid0])
    far1, far0 = swap(far1, outer), swap(mid0, inner)
    mid1 = part(a0, [near0], near_on, [near1])
    last0 = part(a0, [], last_end, [mid1])
    last1 = part(a1, [], last_end, [last0])
    near1, near0 = swap(near1, outer), swap(mid1, inner)
    home0 = part(a0, [far0], home_on, [last1])
    last0, last1 = swap(last0, outer), swap(last1, outer)
    mid0 = part(a1, [far1], far_on, [home0])
    home0, far1 = swap(home0, back), swap(mid0, inner)
    own0 = part(a0, [], all_own, [mid0], jnp.float32)
    mid1 = part(a1, [near1], near_on, [own0])
    near1 = swap(mid1, inner)
    own1 = part(a1, [], all_own, [mid1], jnp.float32)
    home1 = swap(part(a1, [far1], home_on, [own1]), back)
    out = finish([own0, near0, last0, home0], order, me, 0, tok, None)
    return finish([own1, near1, last1, home1], order, me, 1, tok, out)


def per_device(queries, keys, values, w_out, order):
    tok = queries.shape[0]
    half = tok // 2
    line = lax.axis_size("head")
    columns = w_out.shape[1] // line
    me = lax.axis_index("blk").astype(jnp.int32).reshape(1)
    z = lax.axis_index("head").astype(jnp.int32).reshape(1)
    bits = list(range(1, lax.axis_size("blk").bit_length() - 1))
    k_pieces = exchange(keys, "blk", bits + [0])
    v_pieces = exchange(values, "blk", bits[::-1] + [0])

    def attended(chunk, after):
        return attend(queries, k_pieces, v_pieces, order, me, chunk, half, after)

    if line == 4:
        return line_of_four(attended, w_out, z, order, me, columns, tok)
    outs = []
    for c in range(2):
        sums = jnp.dot(attended(c, []), w_out, preferred_element_type=jnp.float32)
        outs.append(lax.psum_scatter(
            sums.astype(jnp.bfloat16), "head", scatter_dimension=1, tiled=True))
    swapped = block_place(0, order, me) == 1
    outs = [jnp.where(swapped, outs[1 - c], outs[c]) for c in range(2)]
    return jnp.concatenate(outs, axis=0)


def solution(mesh):
    return jax.shard_map(
        per_device,
        mesh=mesh,
        in_specs=(P("blk", "head"), P("blk", "head"), P("blk", "head"), P("head", None), P()),
        out_specs=P("blk", "head"),
        check_vma=False,
    )
```

profile of v0, /device:TPU:12, one launch (start us, length us, event | category | flops | bytes accessed | tf_op | source)
XLA Modules:
  0.0 200.3 jit_solution(14131015845181027800)
XLA Ops:
  2.0 1.5 collective-permute-start.3
  4.1 5.3 %collective-permute-done.10.refs_12_ = bf16[512,256]{1,0:T(8,128)(2,1)S(1)} collective-permute-done((bf16[512,256]{1,0:T(8,128)(2,1)}, bf16[512,256]{1,0:T(8,128)(2,1)S(1)}, u32[]{:S(2)}, u32[]{:S(2)}) %collective-permute-start.10) | collective-permute-done | bytes 262176 | tf_op jit(solution)/shard_map/ppermute | solution.py:169
  11.4 2.4 %collective-permute-done.3.refs_4_ = bf16[512,256]{1,0:T(8,128)(2,1)S(1)} collective-permute-done((bf16[512,256]{1,0:T(8,128)(2,1)}, bf16[512,256]{1,0:T(8,128)(2,1)S(1)}, u32[]{:S(2)}, u32[]{:S(2)}) %collective-permute-start.3) | collective-permute-done | bytes 262176 | tf_op jit(solution)/shard_map/ppermute | solution.py:169
  16.2 3.6 %collective-permute-done.12.refs_14_ = bf16[512,256]{1,0:T(8,128)(2,1)S(1)} collective-permute-done((bf16[512,256]{1,0:T(8,128)(2,1)S(1)}, bf16[512,256]{1,0:T(8,128)(2,1)S(1)}, u32[]{:S(2)}, u32[]{:S(2)}) %collective-permute-start.12) | collective-permute-done | bytes 262176 | tf_op jit(solution)/shard_map/ppermute | solution.py:169
  23.7 23.0 %attend.2.a_ref = bf16[256,2048]{1,0:T(8,128)(2,1)S(1)} custom-call(s32[16]{0:T(128)S(1)} %copy-done, s32[1]{0:T(128)} %bitcast.me_ref, bf16[512,2048]{1,0:T(8,128)(2,1)} %q_ref.3, bf16[512,256]{1,0:T(8,128)(2,1)} %refs_0_.3, bf16[512,256]{1,0:T(8,128)(2,1)S(1)} %collective-permute-done.refs_1_, bf16[512,256]{1,0:T(8,128)(2,1)S(1)} %collective-permute-done.1.refs_2_, ...), custom_call_target="tpu_custom_call" | custom-call | flops 1 | tf_op jit(solution)/shard_map/attend/pallas_call | solution.py:139
  46.8 1.7 share.14.refs_0_
  49.8 1.7 share.15.refs_16_
  52.7 24.5 %attend.3.a_ref = bf16[256,2048]{1,0:T(8,128)(2,1)S(1)} custom-call(s32[16]{0:T(128)S(1)} %copy-done, s32[1]{0:T(128)} %bitcast.me_ref, bf16[512,2048]{1,0:T(8,128)(2,1)} %q_ref.3, bf16[512,256]{1,0:T(8,128)(2,1)} %refs_0_.3, bf16[512,256]{1,0:T(8,128)(2,1)S(1)} %collective-permute-done.refs_1_, bf16[512,256]{1,0:T(8,128)(2,1)S(1)} %collective-permute-done.1.refs_2_, ...), custom_call_target="tpu_custom_call" | custom-call | flops 1 | tf_op jit(solution)/shard_map/attend/pallas_call | solution.py:139
  77.3 1.7 share.16.refs_1_
  78.9 5.7 %share.17.refs_0_ = bf16[256,2048]{1,0:T(8,128)(2,1)S(1)} custom-call(s32[1]{0:T(128)} %bitcast.1.z_ref, bf16[256,2048]{1,0:T(8,128)(2,1)S(1)} %attend.2.a_ref, bf16[2048,8192]{1,0:T(8,128)(2,1)} %w_ref.27, bf16[256,2048]{1,0:T(8,128)(2,1)S(1)} %collective-permute-done.14.refs_0_, bf16[256,2048]{1,0:T(8,128)(2,1)S(1)} %share.16.refs_1_), custom_call_target="tpu_custom_call" | custom-call | flops 1 | tf_op jit(solution)/shard_map/share/pallas_call | solution.py:202
  84.7 3.9 %collective-permute-start.17 = (bf16[256,2048]{1,0:T(8,128)(2,1)S(1)}, bf16[256,2048]{1,0:T(8,128)(2,1)S(1)}, u32[]{:S(2)}, u32[]{:S(2)}) collective-permute-start(bf16[256,2048]{1,0:T(8,128)(2,1)S(1)} %share.17.refs_0_), channel_id=1, source_target_pairs={{1,2},{2,1},{5,6},{6,5},{9,10},{10,9},{13,14},{14,13},{17,18},{18,... | collective-permute-start | bytes 3145736 | tf_op jit(solution)/shard_map/ppermute | solution.py:255
  89.9 1.9 share.18.refs_1_
  91.8 8.9 %collective-permute-done.18.refs_0_ = bf16[256,2048]{1,0:T(8,128)(2,1)S(1)} collective-permute-done((bf16[256,2048]{1,0:T(8,128)(2,1)S(1)}, bf16[256,2048]{1,0:T(8,128)(2,1)S(1)}, u32[]{:S(2)}, u32[]{:S(2)}) %collective-permute-start.18) | collective-permute-done | bytes 1048608 | tf_op jit(solution)/shard_map/ppermute | solution.py:255
  100.7 5.7 %share.19.refs_0_ = bf16[256,2048]{1,0:T(8,128)(2,1)S(1)} custom-call(s32[1]{0:T(128)} %bitcast.1.z_ref, bf16[256,2048]{1,0:T(8,128)(2,1)S(1)} %attend.2.a_ref, bf16[2048,8192]{1,0:T(8,128)(2,1)} %w_ref.27, bf16[256,2048]{1,0:T(8,128)(2,1)S(1)} %collective-permute-done.18.refs_0_, bf16[256,2048]{1,0:T(8,128)(2,1)S(1)} %share.18.refs_1_), custom_call_target="tpu_custom_call" | custom-call | flops 1 | tf_op jit(solution)/shard_map/share/pallas_call | solution.py:202
  106.5 1.7 share.20.refs_0_
  109.4 1.7 share.21.refs_1_
  111.7 5.7 %share.22.refs_1_ = bf16[256,2048]{1,0:T(8,128)(2,1)S(1)} custom-call(s32[1]{0:T(128)} %bitcast.1.z_ref, bf16[256,2048]{1,0:T(8,128)(2,1)S(1)} %attend.2.a_ref, bf16[2048,8192]{1,0:T(8,128)(2,1)} %w_ref.27, bf16[256,2048]{1,0:T(8,128)(2,1)S(1)} %collective-permute-done.17.refs_0_, bf16[256,2048]{1,0:T(8,128)(2,1)S(1)} %share.21.refs_1_), custom_call_target="tpu_custom_call" | custom-call | flops 1 | tf_op jit(solution)/shard_map/share/pallas_call | solution.py:202
  117.4 5.8 %collective-permute-done.16.refs_0_ = bf16[256,2048]{1,0:T(8,128)(2,1)S(1)} collective-permute-done((bf16[256,2048]{1,0:T(8,128)(2,1)S(1)}, bf16[256,2048]{1,0:T(8,128)(2,1)S(1)}, u32[]{:S(2)}, u32[]{:S(2)}) %collective-permute-start.16) | collective-permute-done | bytes 1048608 | tf_op jit(solution)/shard_map/ppermute | solution.py:255
  123.2 5.7 %share.23.refs_0_ = bf16[256,2048]{1,0:T(8,128)(2,1)S(1)} custom-call(s32[1]{0:T(128)} %bitcast.1.z_ref, bf16[256,2048]{1,0:T(8,128)(2,1)S(1)} %attend.3.a_ref, bf16[2048,8192]{1,0:T(8,128)(2,1)} %w_ref.27, bf16[256,2048]{1,0:T(8,128)(2,1)S(1)} %collective-permute-done.16.refs_0_, bf16[256,2048]{1,0:T(8,128)(2,1)S(1)} %share.22.refs_1_), custom_call_target="tpu_custom_call" | custom-call | flops 1 | tf_op jit(solution)/shard_map/share/pallas_call | solution.py:202
  128.9 4.6 %collective-permute-start.21 = (bf16[256,2048]{1,0:T(8,128)(2,1)S(1)}, bf16[256,2048]{1,0:T(8,128)(2,1)S(1)}, u32[]{:S(2)}, u32[]{:S(2)}) collective-permute-start(bf16[256,2048]{1,0:T(8,128)(2,1)S(1)} %share.23.refs_0_), channel_id=1, source_target_pairs={{1,2},{2,1},{5,6},{6,5},{9,10},{10,9},{13,14},{14,13},{17,18},{18,... | collective-permute-start | bytes 3145736 | tf_op jit(solution)/shard_map/ppermute | solution.py:255
  134.8 1.9 collective-permute-start.23
  138.1 5.7 %share.24.refs_1_.refs_0_ = f32[256,2048]{1,0:T(8,128)S(1)} custom-call(s32[1]{0:T(128)} %bitcast.1.z_ref, bf16[256,2048]{1,0:T(8,128)(2,1)S(1)} %attend.2.a_ref, bf16[2048,8192]{1,0:T(8,128)(2,1)} %w_ref.27, bf16[256,2048]{1,0:T(8,128)(2,1)S(1)} %share.23.refs_0_), custom_call_target="tpu_custom_call" | custom-call | flops 1 | tf_op jit(solution)/shard_map/share/pallas_call | solution.py:202
  143.7 1.9 collective-permute-done.15.refs_0_
  145.7 5.7 %share.25.refs_0_ = bf16[256,2048]{1,0:T(8,128)(2,1)S(1)} custom-call(s32[1]{0:T(128)} %bitcast.1.z_ref, bf16[256,2048]{1,0:T(8,128)(2,1)S(1)} %attend.3.a_ref, bf16[2048,8192]{1,0:T(8,128)(2,1)} %w_ref.27, bf16[256,2048]{1,0:T(8,128)(2,1)S(1)} %collective-permute-done.15.refs_0_, f32[256,2048]{1,0:T(8,128)S(1)} %share.24.refs_1_.refs_0_), custom_call_target="tpu_custom_call" | custom-call | flops 1 | tf_op jit(solution)/shard_map/share/pallas_call | solution.py:202
  152.8 5.7 %share.26.refs_1_.refs_0_ = f32[256,2048]{1,0:T(8,128)S(1)} custom-call(s32[1]{0:T(128)} %bitcast.1.z_ref, bf16[256,2048]{1,0:T(8,128)(2,1)S(1)} %attend.3.a_ref, bf16[2048,8192]{1,0:T(8,128)(2,1)} %w_ref.27, bf16[256,2048]{1,0:T(8,128)(2,1)S(1)} %share.25.refs_0_), custom_call_target="tpu_custom_call" | custom-call | flops 1 | tf_op jit(solution)/shard_map/share/pallas_call | solution.py:202
  158.5 4.6 %collective-permute-start.19 = (bf16[256,2048]{1,0:T(8,128)(2,1)S(1)}, bf16[256,2048]{1,0:T(8,128)(2,1)S(1)}, u32[]{:S(2)}, u32[]{:S(2)}) collective-permute-start(bf16[256,2048]{1,0:T(8,128)(2,1)S(1)} %share.25.refs_0_), channel_id=1, source_target_pairs={{1,2},{2,1},{5,6},{6,5},{9,10},{10,9},{13,14},{14,13},{17,18},{18,... | collective-permute-start | bytes 3145736 | tf_op jit(solution)/shard_map/ppermute | solution.py:255
  163.1 5.7 %share.27 = bf16[256,2048]{1,0:T(8,128)(2,1)S(1)} custom-call(s32[1]{0:T(128)} %bitcast.1.z_ref, bf16[256,2048]{1,0:T(8,128)(2,1)S(1)} %attend.3.a_ref, bf16[2048,8192]{1,0:T(8,128)(2,1)} %w_ref.27, bf16[256,2048]{1,0:T(8,128)(2,1)S(1)} %collective-permute-done.21.refs_0_, f32[256,2048]{1,0:T(8,128)S(1)} %share.26.refs_1_.refs_0_), custom_call_target="tpu_custom_call" | custom-call | flops 1 | tf_op jit(solution)/shard_map/share/pallas_call | solution.py:202
  170.2 9.9 %collective-permute-done.23.refs_1_ = bf16[256,2048]{1,0:T(8,128)(2,1)S(1)} collective-permute-done((bf16[256,2048]{1,0:T(8,128)(2,1)S(1)}, bf16[256,2048]{1,0:T(8,128)(2,1)S(1)}, u32[]{:S(2)}, u32[]{:S(2)}) %collective-permute-start.23) | collective-permute-done | bytes 1048608 | tf_op jit(solution)/shard_map/ppermute | solution.py:255
  180.1 2.2 %finish.2.refs_4_ = bf16[512,2048]{1,0:T(8,128)(2,1)} custom-call(s32[16]{0:T(128)S(1)} %copy-done.1, s32[1]{0:T(128)} %bitcast.me_ref, f32[256,2048]{1,0:T(8,128)S(1)} %share.24.refs_1_.refs_0_, bf16[256,2048]{1,0:T(8,128)(2,1)S(1)} %collective-permute-done.23.refs_1_, bf16[256,2048]{1,0:T(8,128)(2,1)S(1)} %collective-permute-done.24.refs_2_, ...), custom_call_target="tpu_custom_call" | custom-call | flops 1 | tf_op jit(solution)/shard_map/finish/pallas_call | solution.py:238
  182.3 6.4 %collective-permute-done.20.refs_2_ = bf16[256,2048]{1,0:T(8,128)(2,1)S(1)} collective-permute-done((bf16[256,2048]{1,0:T(8,128)(2,1)S(1)}, bf16[256,2048]{1,0:T(8,128)(2,1)S(1)}, u32[]{:S(2)}, u32[]{:S(2)}) %collective-permute-start.20) | collective-permute-done | bytes 1048608 | tf_op jit(solution)/shard_map/ppermute | solution.py:255
  188.7 9.4 %collective-permute-done.19.refs_1_ = bf16[256,2048]{1,0:T(8,128)(2,1)S(1)} collective-permute-done((bf16[256,2048]{1,0:T(8,128)(2,1)S(1)}, bf16[256,2048]{1,0:T(8,128)(2,1)S(1)}, u32[]{:S(2)}, u32[]{:S(2)}) %collective-permute-start.19) | collective-permute-done | bytes 1048608 | tf_op jit(solution)/shard_map/ppermute | solution.py:255
  198.1 2.2 %finish.3 = bf16[512,2048]{1,0:T(8,128)(2,1)} custom-call(s32[16]{0:T(128)S(1)} %copy-done.1, s32[1]{0:T(128)} %bitcast.me_ref, f32[256,2048]{1,0:T(8,128)S(1)} %share.26.refs_1_.refs_0_, bf16[256,2048]{1,0:T(8,128)(2,1)S(1)} %collective-permute-done.19.refs_1_, ...), custom_call_target="tpu_custom_call", output_to_operand_aliasing={{}: (6, {})} | custom-call | flops 1 | tf_op jit(solution)/shard_map/finish/pallas_call | solution.py:238
  (42 shorter events, 21.9 us)
Async XLA Ops:
  0.0 9.4 %collective-permute-start.10 = (bf16[512,256]{1,0:T(8,128)(2,1)}, bf16[512,256]{1,0:T(8,128)(2,1)S(1)}, u32[]{:S(2)}, u32[]{:S(2)}) collective-permute-start(bf16[512,256]{1,0:T(8,128)(2,1)} %refs_8_.3), channel_id=1, source_target_pairs={{0,16},{4,20},{8,24},{12,28},{16,0},{20,4},{24,8},{28,12},{1,17},{... | collective-permute-start | bytes 786440 | tf_op jit(solution)/shard_map/ppermute | solution.py:169
  0.5 9.4 %collective-permute-start.1 = (bf16[512,256]{1,0:T(8,128)(2,1)}, bf16[512,256]{1,0:T(8,128)(2,1)S(1)}, u32[]{:S(2)}, u32[]{:S(2)}) collective-permute-start(bf16[512,256]{1,0:T(8,128)(2,1)} %refs_0_.3), channel_id=1, source_target_pairs={{0,8},{4,12},{8,0},{12,4},{16,24},{20,28},{24,16},{28,20},{1,9},{5... | collective-permute-start | bytes 786440 | tf_op jit(solution)/shard_map/ppermute | solution.py:169
  2.0 11.9 %collective-permute-start.3 = (bf16[512,256]{1,0:T(8,128)(2,1)}, bf16[512,256]{1,0:T(8,128)(2,1)S(1)}, u32[]{:S(2)}, u32[]{:S(2)}) collective-permute-start(bf16[512,256]{1,0:T(8,128)(2,1)} %refs_0_.3), channel_id=1, source_target_pairs={{0,16},{4,20},{8,24},{12,28},{16,0},{20,4},{24,8},{28,12},{1,17},{... | collective-permute-start | bytes 786440 | tf_op jit(solution)/shard_map/ppermute | solution.py:169
  3.5 12.0 %collective-permute-start.8 = (bf16[512,256]{1,0:T(8,128)(2,1)}, bf16[512,256]{1,0:T(8,128)(2,1)S(1)}, u32[]{:S(2)}, u32[]{:S(2)}) collective-permute-start(bf16[512,256]{1,0:T(8,128)(2,1)} %refs_8_.3), channel_id=1, source_target_pairs={{0,8},{4,12},{8,0},{12,4},{16,24},{20,28},{24,16},{28,20},{1,9},{5... | collective-permute-start | bytes 786440 | tf_op jit(solution)/shard_map/ppermute | solution.py:169
  4.1 11.5 %collective-permute-start = (bf16[512,256]{1,0:T(8,128)(2,1)}, bf16[512,256]{1,0:T(8,128)(2,1)S(1)}, u32[]{:S(2)}, u32[]{:S(2)}) collective-permute-start(bf16[512,256]{1,0:T(8,128)(2,1)} %refs_0_.3), channel_id=1, source_target_pairs={{0,4},{4,0},{8,12},{12,8},{16,20},{20,16},{24,28},{28,24},{1,5},{5... | collective-permute-start | bytes 786440 | tf_op jit(solution)/shard_map/ppermute | solution.py:169
  9.4 6.7 %collective-permute-start.7 = (bf16[512,256]{1,0:T(8,128)(2,1)}, bf16[512,256]{1,0:T(8,128)(2,1)S(1)}, u32[]{:S(2)}, u32[]{:S(2)}) collective-permute-start(bf16[512,256]{1,0:T(8,128)(2,1)} %refs_8_.3), channel_id=1, source_target_pairs={{0,4},{4,0},{8,12},{12,8},{16,20},{20,16},{24,28},{28,24},{1,5},{5... | collective-permute-start | bytes 786440 | tf_op jit(solution)/shard_map/ppermute | solution.py:169
  9.9 9.8 %collective-permute-start.12 = (bf16[512,256]{1,0:T(8,128)(2,1)S(1)}, bf16[512,256]{1,0:T(8,128)(2,1)S(1)}, u32[]{:S(2)}, u32[]{:S(2)}) collective-permute-start(bf16[512,256]{1,0:T(8,128)(2,1)S(1)} %collective-permute-done.10.refs_12_), channel_id=1, source_target_pairs={{0,8},{4,12},{8,0},{12,4},{16,24},{20,28},{24,16},{28,20},{1,9},{5... | collective-permute-start | bytes 786440 | tf_op jit(solution)/shard_map/ppermute | solution.py:169
  13.9 7.2 %collective-permute-start.5 = (bf16[512,256]{1,0:T(8,128)(2,1)S(1)}, bf16[512,256]{1,0:T(8,128)(2,1)S(1)}, u32[]{:S(2)}, u32[]{:S(2)}) collective-permute-start(bf16[512,256]{1,0:T(8,128)(2,1)S(1)} %collective-permute-done.1.refs_2_), channel_id=1, source_target_pairs={{0,16},{4,20},{8,24},{12,28},{16,0},{20,4},{24,8},{28,12},{1,17},{... | collective-permute-start | bytes 786440 | tf_op jit(solution)/shard_map/ppermute | solution.py:169
  15.6 5.5 %collective-permute-start.11 = (bf16[512,256]{1,0:T(8,128)(2,1)S(1)}, bf16[512,256]{1,0:T(8,128)(2,1)S(1)}, u32[]{:S(2)}, u32[]{:S(2)}) collective-permute-start(bf16[512,256]{1,0:T(8,128)(2,1)S(1)} %collective-permute-done.10.refs_12_), channel_id=1, source_target_pairs={{0,4},{4,0},{8,12},{12,8},{16,20},{20,16},{24,28},{28,24},{1,5},{5... | collective-permute-start | bytes 786440 | tf_op jit(solution)/shard_map/ppermute | solution.py:169
  15.6 6.0 %collective-permute-start.2 = (bf16[512,256]{1,0:T(8,128)(2,1)S(1)}, bf16[512,256]{1,0:T(8,128)(2,1)S(1)}, u32[]{:S(2)}, u32[]{:S(2)}) collective-permute-start(bf16[512,256]{1,0:T(8,128)(2,1)S(1)} %collective-permute-done.1.refs_2_), channel_id=1, source_target_pairs={{0,4},{4,0},{8,12},{12,8},{16,20},{20,16},{24,28},{28,24},{1,5},{5... | collective-permute-start | bytes 786440 | tf_op jit(solution)/shard_map/ppermute | solution.py:169
  16.1 5.5 %collective-permute-start.4 = (bf16[512,256]{1,0:T(8,128)(2,1)S(1)}, bf16[512,256]{1,0:T(8,128)(2,1)S(1)}, u32[]{:S(2)}, u32[]{:S(2)}) collective-permute-start(bf16[512,256]{1,0:T(8,128)(2,1)S(1)} %collective-permute-done.3.refs_4_), channel_id=1, source_target_pairs={{0,4},{4,0},{8,12},{12,8},{16,20},{20,16},{24,28},{28,24},{1,5},{5... | collective-permute-start | bytes 786440 | tf_op jit(solution)/shard_map/ppermute | solution.py:169
  19.7 1.9 collective-permute-start.9
  21.1 1.8 collective-permute-start.13
  21.1 2.0 %collective-permute-start.6 = (bf16[512,256]{1,0:T(8,128)(2,1)S(1)}, bf16[512,256]{1,0:T(8,128)(2,1)}, u32[]{:S(2)}, u32[]{:S(2)}) collective-permute-start(bf16[512,256]{1,0:T(8,128)(2,1)S(1)} %collective-permute-done.5.refs_6_), channel_id=1, source_target_pairs={{0,4},{4,0},{8,12},{12,8},{16,20},{20,16},{24,28},{28,24},{1,5},{5... | collective-permute-start | bytes 786440 | tf_op jit(solution)/shard_map/ppermute | solution.py:169
  23.1 0.7 copy-start
  48.5 30.5 %collective-permute-start.14 = (bf16[256,2048]{1,0:T(8,128)(2,1)S(1)}, bf16[256,2048]{1,0:T(8,128)(2,1)S(1)}, u32[]{:S(2)}, u32[]{:S(2)}) collective-permute-start(bf16[256,2048]{1,0:T(8,128)(2,1)S(1)} %share.14.refs_0_), channel_id=1, source_target_pairs={{0,1},{3,2},{4,5},{7,6},{8,9},{11,10},{12,13},{15,14},{16,17},{19,... | collective-permute-start | bytes 3145736 | tf_op jit(solution)/shard_map/ppermute | solution.py:255
  51.4 49.3 %collective-permute-start.18 = (bf16[256,2048]{1,0:T(8,128)(2,1)S(1)}, bf16[256,2048]{1,0:T(8,128)(2,1)S(1)}, u32[]{:S(2)}, u32[]{:S(2)}) collective-permute-start(bf16[256,2048]{1,0:T(8,128)(2,1)S(1)} %share.15.refs_16_), channel_id=1, source_target_pairs={{0,1},{3,2},{4,5},{7,6},{8,9},{11,10},{12,13},{15,14},{16,17},{19,... | collective-permute-start | bytes 3145736 | tf_op jit(solution)/shard_map/ppermute | solution.py:255
  84.7 27.0 %collective-permute-start.17 = (bf16[256,2048]{1,0:T(8,128)(2,1)S(1)}, bf16[256,2048]{1,0:T(8,128)(2,1)S(1)}, u32[]{:S(2)}, u32[]{:S(2)}) collective-permute-start(bf16[256,2048]{1,0:T(8,128)(2,1)S(1)} %share.17.refs_0_), channel_id=1, source_target_pairs={{1,2},{2,1},{5,6},{6,5},{9,10},{10,9},{13,14},{14,13},{17,18},{18,... | collective-permute-start | bytes 3145736 | tf_op jit(solution)/shard_map/ppermute | solution.py:255
  88.6 34.6 %collective-permute-start.16 = (bf16[256,2048]{1,0:T(8,128)(2,1)S(1)}, bf16[256,2048]{1,0:T(8,128)(2,1)S(1)}, u32[]{:S(2)}, u32[]{:S(2)}) collective-permute-start(bf16[256,2048]{1,0:T(8,128)(2,1)S(1)} %share.16.refs_1_), channel_id=1, source_target_pairs={{0,1},{3,2},{4,5},{7,6},{8,9},{11,10},{12,13},{15,14},{16,17},{19,... | collective-permute-start | bytes 3145736 | tf_op jit(solution)/shard_map/ppermute | solution.py:255
  108.1 37.5 %collective-permute-start.15 = (bf16[256,2048]{1,0:T(8,128)(2,1)S(1)}, bf16[256,2048]{1,0:T(8,128)(2,1)S(1)}, u32[]{:S(2)}, u32[]{:S(2)}) collective-permute-start(bf16[256,2048]{1,0:T(8,128)(2,1)S(1)} %share.18.refs_1_), channel_id=1, source_target_pairs={{0,1},{3,2},{4,5},{7,6},{8,9},{11,10},{12,13},{15,14},{16,17},{19,... | collective-permute-start | bytes 3145736 | tf_op jit(solution)/shard_map/ppermute | solution.py:255
  128.9 29.5 %collective-permute-start.21 = (bf16[256,2048]{1,0:T(8,128)(2,1)S(1)}, bf16[256,2048]{1,0:T(8,128)(2,1)S(1)}, u32[]{:S(2)}, u32[]{:S(2)}) collective-permute-start(bf16[256,2048]{1,0:T(8,128)(2,1)S(1)} %share.23.refs_0_), channel_id=1, source_target_pairs={{1,2},{2,1},{5,6},{6,5},{9,10},{10,9},{13,14},{14,13},{17,18},{18,... | collective-permute-start | bytes 3145736 | tf_op jit(solution)/shard_map/ppermute | solution.py:255
  133.5 35.3 %collective-permute-start.24 = (bf16[256,2048]{1,0:T(8,128)(2,1)S(1)}, bf16[256,2048]{1,0:T(8,128)(2,1)S(1)}, u32[]{:S(2)}, u32[]{:S(2)}) collective-permute-start(bf16[256,2048]{1,0:T(8,128)(2,1)S(1)} %share.20.refs_0_), channel_id=1, source_target_pairs={{0,1},{3,2},{4,5},{7,6},{8,9},{11,10},{12,13},{15,14},{16,17},{19,... | collective-permute-start | bytes 3145736 | tf_op jit(solution)/shard_map/ppermute | solution.py:255
  134.8 45.2 %collective-permute-start.23 = (bf16[256,2048]{1,0:T(8,128)(2,1)S(1)}, bf16[256,2048]{1,0:T(8,128)(2,1)S(1)}, u32[]{:S(2)}, u32[]{:S(2)}) collective-permute-start(bf16[256,2048]{1,0:T(8,128)(2,1)S(1)} %share.19.refs_0_), channel_id=1, source_target_pairs={{1,2},{2,1},{5,6},{6,5},{9,10},{10,9},{13,14},{14,13},{17,18},{18,... | collective-permute-start | bytes 3145736 | tf_op jit(solution)/shard_map/ppermute | solution.py:255
  136.8 52.0 %collective-permute-start.20 = (bf16[256,2048]{1,0:T(8,128)(2,1)S(1)}, bf16[256,2048]{1,0:T(8,128)(2,1)S(1)}, u32[]{:S(2)}, u32[]{:S(2)}) collective-permute-start(bf16[256,2048]{1,0:T(8,128)(2,1)S(1)} %share.21.refs_1_), channel_id=1, source_target_pairs={{0,1},{3,2},{4,5},{7,6},{8,9},{11,10},{12,13},{15,14},{16,17},{19,... | collective-permute-start | bytes 3145736 | tf_op jit(solution)/shard_map/ppermute | solution.py:255
  151.4 28.7 %collective-permute-start.25 = (bf16[256,2048]{1,0:T(8,128)(2,1)S(1)}, bf16[256,2048]{1,0:T(8,128)(2,1)S(1)}, u32[]{:S(2)}, u32[]{:S(2)}) collective-permute-start(bf16[256,2048]{1,0:T(8,128)(2,1)S(1)} %share.22.refs_1_), channel_id=1, source_target_pairs={{1,0},{2,3},{5,4},{6,7},{9,8},{10,11},{13,12},{14,15},{17,16},{18,... | collective-permute-start | bytes 3145736 | tf_op jit(solution)/shard_map/ppermute | solution.py:255
  158.4 21.6 %copy-start.1 = (s32[16]{0:T(128)S(1)}, s32[16]{0:T(128)}, u32[]{:S(2)}) copy-start(s32[16]{0:T(128)} %order_ref.7) | copy-start | bytes 196
  158.5 39.6 %collective-permute-start.19 = (bf16[256,2048]{1,0:T(8,128)(2,1)S(1)}, bf16[256,2048]{1,0:T(8,128)(2,1)S(1)}, u32[]{:S(2)}, u32[]{:S(2)}) collective-permute-start(bf16[256,2048]{1,0:T(8,128)(2,1)S(1)} %share.25.refs_0_), channel_id=1, source_target_pairs={{1,2},{2,1},{5,6},{6,5},{9,10},{10,9},{13,14},{14,13},{17,18},{18,... | collective-permute-start | bytes 3145736 | tf_op jit(solution)/shard_map/ppermute | solution.py:255
  168.9 29.3 %collective-permute-start.22 = (bf16[256,2048]{1,0:T(8,128)(2,1)S(1)}, bf16[256,2048]{1,0:T(8,128)(2,1)S(1)}, u32[]{:S(2)}, u32[]{:S(2)}) collective-permute-start(bf16[256,2048]{1,0:T(8,128)(2,1)S(1)} %share.27), channel_id=1, source_target_pairs={{1,0},{2,3},{5,4},{6,7},{9,8},{10,11},{13,12},{14,15},{17,16},{18,... | collective-permute-start | bytes 3145736 | tf_op jit(solution)/shard_map/ppermute | solution.py:255
where the time goes:
time: 198 us; the launch traced here: 200 us
  Pallas kernels  108 us (55%)
  waiting for transfers between devices  58.9 us (30%)
  starting transfers between devices  32.7 us (17%)
    pallas_call x14, Pallas kernels, share(): pl.pallas_call(functools.partial(share_kernel, extra, blocks), out_shape=...  55.9 us
    pallas_call x2, Pallas kernels, attend(): pl.pallas_call(functools.partial(attend_kernel, half, tile, chunk, pieces...  47.5 us
    ppermute x12, waiting for transfers between devices, swap(): return lax.ppermute(array, 'head', pairs)  42.9 us
    ppermute x12, starting transfers between devices, swap(): return lax.ppermute(array, 'head', pairs)  25.5 us
    ppermute x14, waiting for transfers between devices, exchange(): lax.ppermute(a, axis, pairs)  15.9 us
    ppermute x14, starting transfers between devices, exchange(): lax.ppermute(a, axis, pairs)  7.15 us
    pallas_call x2, Pallas kernels, finish(): pl.pallas_call(functools.partial(finish_kernel, len(terms)), out_shape=ja...  4.42 us
  transfers between devices with their start and end apart: 26, of which 15 were waited for; matrix products, arithmetic and copies ran while one was open for 0% of the time, Pallas kernels for 40%

commit v1 on v0

--- a/solution.py
+++ b/solution.py
@@ -23,34 +23,53 @@
     return jnp.where(order_ref[own] > order_ref[own + 1], 1 - chunk, chunk)
 
 
-def attend_kernel(half, tile, chunk, pieces, waited, order_ref, me_ref, q_ref, *refs):
+def attend_kernel(half, chunk, pieces, heads, waited, order_ref, me_ref, q_ref, *refs):
     k_refs, v_refs = refs[:pieces], refs[pieces:2 * pieces]
-    o_ref, inv, q_rows, k_all, v_wide, acc, top = refs[2 * pieces + waited:]
+    o_ref, inv, q_heads, k_all, v_wide, acc, top, sems = refs[2 * pieces + waited:]
     blocks = order_ref.shape[0]
     per = blocks // pieces
-    tok = q_ref.shape[0]
-    group = q_ref.shape[1] // HD
-    rows = group * tok
+    tile = half
+    width = o_ref.shape[1]
+    group = width // HD
     shard = per * half
     factor = HD ** (-0.5) * math.log2(math.e)
     own = block_place(chunk, order_ref, me_ref)
     me = me_ref[0]
+    head = pl.program_id(0)
+
+    def copies(h):
+        rows = pl.ds(pl.multiple_of(own * half, half), half)
+        pairs = [(q_ref.at[rows, pl.ds(h * width, width)], q_heads.at[h])]
+        for r in range(pieces):
+            here = pl.ds(r * shard, shard)
+            lanes = pl.ds(h * HD, HD)
+            pairs.append((k_refs[r].at[:, lanes], k_all.at[h, here, :]))
+            pairs.append((v_refs[r].at[:, lanes], v_wide.at[h, here, pl.ds(0, HD)]))
+        return [pltpu.make_async_copy(src, dst, sems.at[h, i])
+                for i, (src, dst) in enumerate(pairs)]
+
+    @pl.when(head == 0)
+    def _():
+        for h in range(heads):
+            for copy in copies(h):
+                copy.start()
 
     def invert(b, _):
         inv[order_ref[b]] = jnp.bitwise_xor(b // per, me) * per + lax.rem(b, per)
         return 0
 
     lax.fori_loop(0, blocks, invert, 0)
-    for g in range(group):
-        q_rows[g * tok:(g + 1) * tok, :] = q_ref[:, g * HD:(g + 1) * HD]
-    for r in range(pieces):
-        k_all[r * shard:(r + 1) * shard, :] = k_refs[r][...]
-        v_wide[r * shard:(r + 1) * shard, :HD] = v_refs[r][...]
-    v_wide[:, HD:] = jnp.ones((v_wide.shape[0], HD), v_wide.dtype)
+    v_wide[head, :, HD:] = jnp.ones((v_wide.shape[1], HD), v_wide.dtype)
+    for h in range(heads):
+        @pl.when(head == h)
+        def _():
+            for copy in copies(h):
+                copy.wait()
+
     earlier = order_ref[me * per + own]
 
     def block_of(ref, b):
-        return ref[pl.ds(pl.multiple_of(b * half, half), half), :]
+        return ref[head, pl.ds(pl.multiple_of(b * half, half), half), :]
 
     def first(blocks_in):
         k_cat = jnp.concatenate([block_of(k_all, b) for b in blocks_in], axis=0)
@@ -74,19 +93,19 @@
                 jnp.concatenate([block_of(v_wide, b) for b in blocks_in], axis=0))
 
     def over_tiles(k_cat, use):
-        def scores(r):
-            return lax.dot_general(q_rows[r:r + tile, :], k_cat, NT,
+        def scores(g):
+            return lax.dot_general(q_heads[head, :, g * HD:(g + 1) * HD], k_cat, NT,
                                    preferred_element_type=jnp.float32)
 
         score = scores(0)
-        for r in range(0, rows, tile):
-            ahead = scores(r + tile) if r + tile < rows else None
-            use(r, score)
+        for g in range(group):
+            ahead = scores(g + 1) if g + 1 < group else None
+            use(g * tile, score)
             score = ahead
 
     def first(rest):
         k_cat, v_cat = keys_of([inv[earlier - rest + i] for i in range(rest)] + [own])
-        query = lax.rem(lax.broadcasted_iota(jnp.int32, (tile, half), 0), tok)
+        query = lax.broadcasted_iota(jnp.int32, (tile, half), 0)
         seen = lax.broadcasted_iota(jnp.int32, (tile, half), 1) <= query
 
         def use(r, score):
@@ -122,43 +141,41 @@
 
     lax.fori_loop(0, earlier // STEP, step, 0)
     for g in range(group):
-        part = acc[g * tok:(g + 1) * tok, :]
+        part = acc[g * tile:(g + 1) * tile, :]
         o_ref[:, g * HD:(g + 1) * HD] = (part[:, :HD] / part[:, HD:]).astype(o_ref.dtype)
 
 
 def attend(queries, k_pieces, v_pieces, order, me, chunk, half, after=()):
-    tok = half
     pieces = len(k_pieces)
     shard, kv_width = k_pieces[0].shape
-    kv_local = kv_width // HD
-    width = queries.shape[1] // kv_local
+    heads = kv_width // HD
+    width = queries.shape[1] // heads
     keys = shard * pieces
-    rows = width // HD * tok
-    tile = min(rows, 256)
-    piece_spec = pl.BlockSpec((shard, HD), lambda h, *_: (0, h))
+    rows = width // HD * half
+    anywhere = pl.BlockSpec(memory_space=pl.ANY)
     return pl.pallas_call(
-        functools.partial(attend_kernel, half, tile, chunk, pieces, len(after)),
-        out_shape=jax.ShapeDtypeStruct((tok, queries.shape[1]), jnp.bfloat16),
+        functools.partial(attend_kernel, half, chunk, pieces, heads, len(after)),
+        out_shape=jax.ShapeDtypeStruct((half, queries.shape[1]), jnp.bfloat16),
         grid_spec=pltpu.PrefetchScalarGridSpec(
             num_scalar_prefetch=2,
-            grid=(kv_local,),
-            in_specs=[pl.BlockSpec((tok, width), lambda h, *refs: (block_place(chunk, *refs), h))]
-            + [piece_spec] * (2 * pieces)
-            + [pl.BlockSpec(memory_space=pl.ANY)] * len(after),
-            out_specs=pl.BlockSpec((tok, width), lambda h, *_: (0, h)),
+            grid=(heads,),
+            in_specs=[anywhere] * (1 + 2 * pieces + len(after)),
+            out_specs=pl.BlockSpec((half, width), lambda h, *_: (0, h)),
             scratch_shapes=[
                 pltpu.SMEM((order.shape[0],), jnp.int32),
-                pltpu.VMEM((rows, HD), jnp.bfloat16),
-                pltpu.VMEM((keys, HD), jnp.bfloat16),
-                pltpu.VMEM((keys, 2 * HD), jnp.bfloat16),
+                pltpu.VMEM((heads, half, width), jnp.bfloat16),
+                pltpu.VMEM((heads, keys, HD), jnp.bfloat16),
+                pltpu.VMEM((heads, keys, 2 * HD), jnp.bfloat16),
                 pltpu.VMEM((rows, 2 * HD), jnp.float32),
                 pltpu.VMEM((rows, HD), jnp.float32),
+                pltpu.SemaphoreType.DMA((heads, 2 * pieces + 1)),
             ],
         ),
         compiler_params=pltpu.CompilerParams(vmem_limit_bytes=40 * MIB),
         cost_estimate=pl.CostEstimate(flops=1, bytes_accessed=0, transcendentals=0),
         name="attend",
-    )(order, me, in_hbm(queries), in_hbm(k_pieces[0]), *k_pieces[1:], in_hbm(v_pieces[0]), *v_pieces[1:], *after)
+    )(order, me, in_hbm(queries), in_hbm(k_pieces[0]), *k_pieces[1:],
+      in_hbm(v_pieces[0]), *v_pieces[1:], *after)
 
 
 def exchange(arrays, axis, bits):
@@ -177,40 +194,51 @@
     return value
 
 
-def share_kernel(extra, blocks, z_ref, a_ref, w_ref, *refs):
-    @pl.when(pick(z_ref[0], blocks) >= 0)
+def share_kernel(extra, waited, blocks, z_ref, a_ref, w_ref, *refs):
+    arrived = refs[:extra]
+    out, tiles, sems = refs[extra + waited:]
+    count, _, wide = tiles.shape
+    block = pick(z_ref[0], blocks)
+
+    @pl.when(block >= 0)
     def _():
-        total = jnp.dot(a_ref[...], w_ref[...], preferred_element_type=jnp.float32)
-        for ref in refs[:extra]:
-            total = total + ref[...].astype(jnp.float32)
-        refs[-1][...] = total.astype(refs[-1].dtype)
+        def copy(j):
+            place = pl.multiple_of((block * count + j) * wide, wide)
+            return pltpu.make_async_copy(w_ref.at[:, pl.ds(place, wide)], tiles.at[j], sems.at[j])
+
+        def column(j, _):
+            copy(j).wait()
+            lanes = pl.ds(pl.multiple_of(j * wide, wide), wide)
+            total = jnp.dot(a_ref[...], tiles[j], preferred_element_type=jnp.float32)
+            for ref in arrived:
+                total = total + ref[:, lanes].astype(jnp.float32)
+            out[:, lanes] = total.astype(out.dtype)
+            return 0
+
+        for j in range(count):
+            copy(j).start()
+        lax.fori_loop(0, count, column, 0)
 
 
 def share(attended, w_out, arrived, z, blocks, columns, after=(), kind=jnp.bfloat16):
     tok, depth = attended.shape
-    wide = min(columns, 512)
-    tiles = columns // wide
+    wide = min(columns, 256)
+    count = columns // wide
     extra = len(arrived)
-
-    def at(j, z_ref):
-        block = pick(z_ref[0], blocks)
-        return (0, jnp.maximum(block, 0) * tiles + jnp.where(block >= 0, j, 0))
-
-    def inside(j, z_ref):
-        return (0, jnp.where(pick(z_ref[0], blocks) >= 0, j, 0))
-
+    whole = pl.BlockSpec(memory_space=pltpu.VMEM)
+    anywhere = pl.BlockSpec(memory_space=pl.ANY)
     return pl.pallas_call(
-        functools.partial(share_kernel, extra, blocks),
+        functools.partial(share_kernel, extra, len(after), blocks),
         out_shape=jax.ShapeDtypeStruct((tok, columns), kind),
         grid_spec=pltpu.PrefetchScalarGridSpec(
             num_scalar_prefetch=1,
-            grid=(tiles,),
-            in_specs=[
-                pl.BlockSpec((tok, depth), lambda j, z_ref: (0, 0)),
-                pl.BlockSpec((depth, wide), at),
-            ] + [pl.BlockSpec((tok, wide), inside)] * extra
-            + [pl.BlockSpec(memory_space=pl.ANY)] * len(after),
-            out_specs=pl.BlockSpec((tok, wide), inside),
+            grid=(),
+            in_specs=[whole, anywhere] + [whole] * extra + [anywhere] * len(after),
+            out_specs=whole,
+            scratch_shapes=[
+                pltpu.VMEM((count, depth, wide), w_out.dtype),
+                pltpu.SemaphoreType.DMA((count,)),
+            ],
         ),
         compiler_params=pltpu.CompilerParams(vmem_limit_bytes=40 * MIB),
         cost_estimate=pl.CostEstimate(flops=1, bytes_accessed=0, transcendentals=0),
@@ -283,7 +311,7 @@
     own0 = part(a0, [], all_own, [mid0], jnp.float32)
     mid1 = part(a1, [near1], near_on, [own0])
     near1 = swap(mid1, inner)
-    own1 = part(a1, [], all_own, [mid1], jnp.float32)
+    own1 = part(a1, [], all_own, [mid1, near0, home0], jnp.float32)
     home1 = swap(part(a1, [far1], home_on, [own1]), back)
     out = finish([own0, near0, last0, home0], order, me, 0, tok, None)
     return finish([own1, near1, last1, home1], order, me, 1, tok, out)

time: 198 us -> 182 us (0.919)
  the two profiles are of different devices: /device:TPU:12 before, /device:TPU:19 now
where the time goes in v1:
time: 182 us; the launch traced here: 181 us
  Pallas kernels  90.5 us (50%)
  waiting for transfers between devices  53.5 us (29%)
  starting transfers between devices  35.7 us (20%)
    pallas_call x2, Pallas kernels, attend(): pl.pallas_call(functools.partial(attend_kernel, half, chunk, pieces, head...  45.3 us
    ppermute x12, waiting for transfers between devices, swap(): return lax.ppermute(array, 'head', pairs)  44.8 us
    pallas_call x14, Pallas kernels, share(): pl.pallas_call(functools.partial(share_kernel, extra, len(after), blocks)...  40.8 us
    ppermute x12, starting transfers between devices, swap(): return lax.ppermute(array, 'head', pairs)  20.9 us
    ppermute x14, starting transfers between devices, exchange(): lax.ppermute(a, axis, pairs)  14.8 us
    ppermute x14, waiting for transfers between devices, exchange(): lax.ppermute(a, axis, pairs)  8.63 us
    pallas_call x2, Pallas kernels, finish(): pl.pallas_call(functools.partial(finish_kernel, len(terms)), out_shape=ja...  4.42 us
  transfers between devices with their start and end apart: 26, of which 12 were waited for; matrix products, arithmetic and copies ran while one was open for 0% of the time, Pallas kernels for 37%

profile of v1, /device:TPU:19, one launch (start us, length us, event | category | flops | bytes accessed | tf_op | source)
XLA Modules:
  0.0 180.6 jit_solution(16957485924073868175)
XLA Ops:
  2.9 1.8 collective-permute-start
  4.7 2.7 %collective-permute-done.10.refs_12_ = bf16[512,256]{1,0:T(8,128)(2,1)S(1)} collective-permute-done((bf16[512,256]{1,0:T(8,128)(2,1)}, bf16[512,256]{1,0:T(8,128)(2,1)S(1)}, u32[]{:S(2)}, u32[]{:S(2)}) %collective-permute-start.10) | collective-permute-done | bytes 262176 | tf_op jit(solution)/shard_map/ppermute | solution.py:186
  7.4 2.7 %collective-permute-start.7 = (bf16[512,256]{1,0:T(8,128)(2,1)}, bf16[512,256]{1,0:T(8,128)(2,1)S(1)}, u32[]{:S(2)}, u32[]{:S(2)}) collective-permute-start(bf16[512,256]{1,0:T(8,128)(2,1)} %refs_8_.3), channel_id=1, source_target_pairs={{0,4},{4,0},{8,12},{12,8},{16,20},{20,16},{24,28},{28,24},{1,5},{5... | collective-permute-start | bytes 786440 | tf_op jit(solution)/shard_map/ppermute | solution.py:186
  10.3 2.7 %collective-permute-done.3.refs_4_ = bf16[512,256]{1,0:T(8,128)(2,1)S(1)} collective-permute-done((bf16[512,256]{1,0:T(8,128)(2,1)}, bf16[512,256]{1,0:T(8,128)(2,1)S(1)}, u32[]{:S(2)}, u32[]{:S(2)}) %collective-permute-start.3) | collective-permute-done | bytes 262176 | tf_op jit(solution)/shard_map/ppermute | solution.py:186
  14.2 3.0 %collective-permute-start.11 = (bf16[512,256]{1,0:T(8,128)(2,1)S(1)}, bf16[512,256]{1,0:T(8,128)(2,1)S(1)}, u32[]{:S(2)}, u32[]{:S(2)}) collective-permute-start(bf16[512,256]{1,0:T(8,128)(2,1)S(1)} %collective-permute-done.10.refs_12_), channel_id=1, source_target_pairs={{0,4},{4,0},{8,12},{12,8},{16,20},{20,16},{24,28},{28,24},{1,5},{5... | collective-permute-start | bytes 786440 | tf_op jit(solution)/shard_map/ppermute | solution.py:186
  17.8 1.8 collective-permute-done.12.refs_14_
  19.5 1.9 %collective-permute-start.9 = (bf16[512,256]{1,0:T(8,128)(2,1)S(1)}, bf16[512,256]{1,0:T(8,128)(2,1)S(1)}, u32[]{:S(2)}, u32[]{:S(2)}) collective-permute-start(bf16[512,256]{1,0:T(8,128)(2,1)S(1)} %collective-permute-done.8.refs_10_), channel_id=1, source_target_pairs={{0,4},{4,0},{8,12},{12,8},{16,20},{20,16},{24,28},{28,24},{1,5},{5... | collective-permute-start | bytes 786440 | tf_op jit(solution)/shard_map/ppermute | solution.py:186
  24.1 21.4 %attend.2.a_ref = bf16[256,2048]{1,0:T(8,128)(2,1)S(1)} custom-call(s32[16]{0:T(128)S(1)} %copy-done, s32[1]{0:T(128)} %bitcast.me_ref, bf16[512,2048]{1,0:T(8,128)(2,1)} %q_ref.3, bf16[512,256]{1,0:T(8,128)(2,1)} %refs_0_.3, bf16[512,256]{1,0:T(8,128)(2,1)S(1)} %collective-permute-done.refs_1_, bf16[512,256]{1,0:T(8,128)(2,1)S(1)} %collective-permute-done.1.refs_2_, ...), custom_call_target="tpu_custom_call" | custom-call | flops 1 | tf_op jit(solution)/shard_map/attend/pallas_call | solution.py:156
  47.1 1.3 collective-permute-start.18
  48.4 23.9 %attend.3.a_ref = bf16[256,2048]{1,0:T(8,128)(2,1)S(1)} custom-call(s32[16]{0:T(128)S(1)} %copy-done, s32[1]{0:T(128)} %bitcast.me_ref, bf16[512,2048]{1,0:T(8,128)(2,1)} %q_ref.3, bf16[512,256]{1,0:T(8,128)(2,1)} %refs_0_.3, bf16[512,256]{1,0:T(8,128)(2,1)S(1)} %collective-permute-done.refs_1_, bf16[512,256]{1,0:T(8,128)(2,1)S(1)} %collective-permute-done.1.refs_2_, ...), custom_call_target="tpu_custom_call" | custom-call | flops 1 | tf_op jit(solution)/shard_map/attend/pallas_call | solution.py:156
  72.7 4.3 %collective-permute-done.14.refs_0_ = bf16[256,2048]{1,0:T(8,128)(2,1)S(1)} collective-permute-done((bf16[256,2048]{1,0:T(8,128)(2,1)S(1)}, bf16[256,2048]{1,0:T(8,128)(2,1)S(1)}, u32[]{:S(2)}, u32[]{:S(2)}) %collective-permute-start.14) | collective-permute-done | bytes 1048608 | tf_op jit(solution)/shard_map/ppermute | solution.py:283
  77.0 5.0 %share.17.refs_0_ = bf16[256,2048]{1,0:T(8,128)(2,1)S(1)} custom-call(s32[1]{0:T(128)} %bitcast.1.z_ref, bf16[256,2048]{1,0:T(8,128)(2,1)S(1)} %attend.2.a_ref, bf16[2048,8192]{1,0:T(8,128)(2,1)} %w_ref.27, bf16[256,2048]{1,0:T(8,128)(2,1)S(1)} %collective-permute-done.14.refs_0_, bf16[256,2048]{1,0:T(8,128)(2,1)S(1)} %share.16.refs_1_), custom_call_target="tpu_custom_call" | custom-call | flops 1 | tf_op jit(solution)/shard_map/share/pallas_call | solution.py:230
  82.0 1.9 %collective-permute-start.17 = (bf16[256,2048]{1,0:T(8,128)(2,1)S(1)}, bf16[256,2048]{1,0:T(8,128)(2,1)S(1)}, u32[]{:S(2)}, u32[]{:S(2)}) collective-permute-start(bf16[256,2048]{1,0:T(8,128)(2,1)S(1)} %share.17.refs_0_), channel_id=1, source_target_pairs={{1,2},{2,1},{5,6},{6,5},{9,10},{10,9},{13,14},{14,13},{17,18},{18,... | collective-permute-start | bytes 3145736 | tf_op jit(solution)/shard_map/ppermute | solution.py:283
  85.3 14.2 %collective-permute-done.18.refs_0_ = bf16[256,2048]{1,0:T(8,128)(2,1)S(1)} collective-permute-done((bf16[256,2048]{1,0:T(8,128)(2,1)S(1)}, bf16[256,2048]{1,0:T(8,128)(2,1)S(1)}, u32[]{:S(2)}, u32[]{:S(2)}) %collective-permute-start.18) | collective-permute-done | bytes 1048608 | tf_op jit(solution)/shard_map/ppermute | solution.py:283
  99.5 5.0 %share.19.refs_0_ = bf16[256,2048]{1,0:T(8,128)(2,1)S(1)} custom-call(s32[1]{0:T(128)} %bitcast.1.z_ref, bf16[256,2048]{1,0:T(8,128)(2,1)S(1)} %attend.2.a_ref, bf16[2048,8192]{1,0:T(8,128)(2,1)} %w_ref.27, bf16[256,2048]{1,0:T(8,128)(2,1)S(1)} %collective-permute-done.18.refs_0_, bf16[256,2048]{1,0:T(8,128)(2,1)S(1)} %share.18.refs_1_), custom_call_target="tpu_custom_call" | custom-call | flops 1 | tf_op jit(solution)/shard_map/share/pallas_call | solution.py:230
  104.6 1.9 %collective-permute-start.19 = (bf16[256,2048]{1,0:T(8,128)(2,1)S(1)}, bf16[256,2048]{1,0:T(8,128)(2,1)S(1)}, u32[]{:S(2)}, u32[]{:S(2)}) collective-permute-start(bf16[256,2048]{1,0:T(8,128)(2,1)S(1)} %share.19.refs_0_), channel_id=1, source_target_pairs={{1,2},{2,1},{5,6},{6,5},{9,10},{10,9},{13,14},{14,13},{17,18},{18,... | collective-permute-start | bytes 3145736 | tf_op jit(solution)/shard_map/ppermute | solution.py:283
  107.9 5.0 %share.22.refs_1_ = bf16[256,2048]{1,0:T(8,128)(2,1)S(1)} custom-call(s32[1]{0:T(128)} %bitcast.1.z_ref, bf16[256,2048]{1,0:T(8,128)(2,1)S(1)} %attend.2.a_ref, bf16[2048,8192]{1,0:T(8,128)(2,1)} %w_ref.27, bf16[256,2048]{1,0:T(8,128)(2,1)S(1)} %collective-permute-done.17.refs_0_, bf16[256,2048]{1,0:T(8,128)(2,1)S(1)} %share.21.refs_1_), custom_call_target="tpu_custom_call" | custom-call | flops 1 | tf_op jit(solution)/shard_map/share/pallas_call | solution.py:230
  112.9 4.1 %collective-permute-start.20 = (bf16[256,2048]{1,0:T(8,128)(2,1)S(1)}, bf16[256,2048]{1,0:T(8,128)(2,1)S(1)}, u32[]{:S(2)}, u32[]{:S(2)}) collective-permute-start(bf16[256,2048]{1,0:T(8,128)(2,1)S(1)} %share.22.refs_1_), channel_id=1, source_target_pairs={{1,0},{2,3},{5,4},{6,7},{9,8},{10,11},{13,12},{14,15},{17,16},{18,... | collective-permute-start | bytes 3145736 | tf_op jit(solution)/shard_map/ppermute | solution.py:283
  117.0 4.9 %collective-permute-done.16.refs_0_ = bf16[256,2048]{1,0:T(8,128)(2,1)S(1)} collective-permute-done((bf16[256,2048]{1,0:T(8,128)(2,1)S(1)}, bf16[256,2048]{1,0:T(8,128)(2,1)S(1)}, u32[]{:S(2)}, u32[]{:S(2)}) %collective-permute-start.16) | collective-permute-done | bytes 1048608 | tf_op jit(solution)/shard_map/ppermute | solution.py:283
  122.0 5.0 %share.23.refs_0_ = bf16[256,2048]{1,0:T(8,128)(2,1)S(1)} custom-call(s32[1]{0:T(128)} %bitcast.1.z_ref, bf16[256,2048]{1,0:T(8,128)(2,1)S(1)} %attend.3.a_ref, bf16[2048,8192]{1,0:T(8,128)(2,1)} %w_ref.27, bf16[256,2048]{1,0:T(8,128)(2,1)S(1)} %collective-permute-done.16.refs_0_, bf16[256,2048]{1,0:T(8,128)(2,1)S(1)} %share.22.refs_1_), custom_call_target="tpu_custom_call" | custom-call | flops 1 | tf_op jit(solution)/shard_map/share/pallas_call | solution.py:230
  127.0 1.9 %collective-permute-start.23 = (bf16[256,2048]{1,0:T(8,128)(2,1)S(1)}, bf16[256,2048]{1,0:T(8,128)(2,1)S(1)}, u32[]{:S(2)}, u32[]{:S(2)}) collective-permute-start(bf16[256,2048]{1,0:T(8,128)(2,1)S(1)} %share.23.refs_0_), channel_id=1, source_target_pairs={{1,2},{2,1},{5,6},{6,5},{9,10},{10,9},{13,14},{14,13},{17,18},{18,... | collective-permute-start | bytes 3145736 | tf_op jit(solution)/shard_map/ppermute | solution.py:283
  130.2 5.0 %share.24.refs_1_.refs_0_ = f32[256,2048]{1,0:T(8,128)S(1)} custom-call(s32[1]{0:T(128)} %bitcast.1.z_ref, bf16[256,2048]{1,0:T(8,128)(2,1)S(1)} %attend.2.a_ref, bf16[2048,8192]{1,0:T(8,128)(2,1)} %w_ref.27, bf16[256,2048]{1,0:T(8,128)(2,1)S(1)} %share.23.refs_0_), custom_call_target="tpu_custom_call" | custom-call | flops 1 | tf_op jit(solution)/shard_map/share/pallas_call | solution.py:230
  135.2 9.3 %collective-permute-done.15.refs_0_ = bf16[256,2048]{1,0:T(8,128)(2,1)S(1)} collective-permute-done((bf16[256,2048]{1,0:T(8,128)(2,1)S(1)}, bf16[256,2048]{1,0:T(8,128)(2,1)S(1)}, u32[]{:S(2)}, u32[]{:S(2)}) %collective-permute-start.15) | collective-permute-done | bytes 1048608 | tf_op jit(solution)/shard_map/ppermute | solution.py:283
  145.7 5.0 %share.25.refs_0_ = bf16[256,2048]{1,0:T(8,128)(2,1)S(1)} custom-call(s32[1]{0:T(128)} %bitcast.1.z_ref, bf16[256,2048]{1,0:T(8,128)(2,1)S(1)} %attend.3.a_ref, bf16[2048,8192]{1,0:T(8,128)(2,1)} %w_ref.27, bf16[256,2048]{1,0:T(8,128)(2,1)S(1)} %collective-permute-done.15.refs_0_, f32[256,2048]{1,0:T(8,128)S(1)} %share.24.refs_1_.refs_0_), custom_call_target="tpu_custom_call" | custom-call | flops 1 | tf_op jit(solution)/shard_map/share/pallas_call | solution.py:230
  150.7 1.9 %collective-permute-start.21 = (bf16[256,2048]{1,0:T(8,128)(2,1)S(1)}, bf16[256,2048]{1,0:T(8,128)(2,1)S(1)}, u32[]{:S(2)}, u32[]{:S(2)}) collective-permute-start(bf16[256,2048]{1,0:T(8,128)(2,1)S(1)} %share.25.refs_0_), channel_id=1, source_target_pairs={{1,2},{2,1},{5,6},{6,5},{9,10},{10,9},{13,14},{14,13},{17,18},{18,... | collective-permute-start | bytes 3145736 | tf_op jit(solution)/shard_map/ppermute | solution.py:283
  152.7 5.0 %share.26.refs_1_.refs_0_ = f32[256,2048]{1,0:T(8,128)S(1)} custom-call(s32[1]{0:T(128)} %bitcast.1.z_ref, bf16[256,2048]{1,0:T(8,128)(2,1)S(1)} %attend.3.a_ref, bf16[2048,8192]{1,0:T(8,128)(2,1)} %w_ref.27, bf16[256,2048]{1,0:T(8,128)(2,1)S(1)} %share.25.refs_0_, bf16[256,2048]{1,0:T(8,128)(2,1)S(1)} %collective-permute-done.19.refs_1_, ...), custom_call_target="tpu_custom_call" | custom-call | flops 1 | tf_op jit(solution)/shard_map/share/pallas_call | solution.py:230
  157.7 5.0 %share.27 = bf16[256,2048]{1,0:T(8,128)(2,1)S(1)} custom-call(s32[1]{0:T(128)} %bitcast.1.z_ref, bf16[256,2048]{1,0:T(8,128)(2,1)S(1)} %attend.3.a_ref, bf16[2048,8192]{1,0:T(8,128)(2,1)} %w_ref.27, bf16[256,2048]{1,0:T(8,128)(2,1)S(1)} %collective-permute-done.23.refs_0_, f32[256,2048]{1,0:T(8,128)S(1)} %share.26.refs_1_.refs_0_), custom_call_target="tpu_custom_call" | custom-call | flops 1 | tf_op jit(solution)/shard_map/share/pallas_call | solution.py:230
  162.7 1.4 collective-permute-start.24
  164.1 2.8 %collective-permute-done.25.refs_2_ = bf16[256,2048]{1,0:T(8,128)(2,1)S(1)} collective-permute-done((bf16[256,2048]{1,0:T(8,128)(2,1)S(1)}, bf16[256,2048]{1,0:T(8,128)(2,1)S(1)}, u32[]{:S(2)}, u32[]{:S(2)}) %collective-permute-start.25) | collective-permute-done | bytes 1048608 | tf_op jit(solution)/shard_map/ppermute | solution.py:283
  166.9 2.2 %finish.2.refs_4_ = bf16[512,2048]{1,0:T(8,128)(2,1)} custom-call(s32[16]{0:T(128)S(1)} %copy-done.1, s32[1]{0:T(128)} %bitcast.me_ref, f32[256,2048]{1,0:T(8,128)S(1)} %share.24.refs_1_.refs_0_, bf16[256,2048]{1,0:T(8,128)(2,1)S(1)} %collective-permute-done.19.refs_1_, bf16[256,2048]{1,0:T(8,128)(2,1)S(1)} %collective-permute-done.25.refs_2_, ...), custom_call_target="tpu_custom_call" | custom-call | flops 1 | tf_op jit(solution)/shard_map/finish/pallas_call | solution.py:266
  169.1 9.3 %collective-permute-done.22.refs_2_ = bf16[256,2048]{1,0:T(8,128)(2,1)S(1)} collective-permute-done((bf16[256,2048]{1,0:T(8,128)(2,1)S(1)}, bf16[256,2048]{1,0:T(8,128)(2,1)S(1)}, u32[]{:S(2)}, u32[]{:S(2)}) %collective-permute-start.22) | collective-permute-done | bytes 1048608 | tf_op jit(solution)/shard_map/ppermute | solution.py:283
  178.4 2.2 %finish.3 = bf16[512,2048]{1,0:T(8,128)(2,1)} custom-call(s32[16]{0:T(128)S(1)} %copy-done.1, s32[1]{0:T(128)} %bitcast.me_ref, f32[256,2048]{1,0:T(8,128)S(1)} %share.26.refs_1_.refs_0_, bf16[256,2048]{1,0:T(8,128)(2,1)S(1)} %collective-permute-done.21.refs_1_, ...), custom_call_target="tpu_custom_call", output_to_operand_aliasing={{}: (6, {})} | custom-call | flops 1 | tf_op jit(solution)/shard_map/finish/pallas_call | solution.py:266
  (42 shorter events, 15.0 us)
Async XLA Ops:
  0.0 7.4 %collective-permute-start.10 = (bf16[512,256]{1,0:T(8,128)(2,1)}, bf16[512,256]{1,0:T(8,128)(2,1)S(1)}, u32[]{:S(2)}, u32[]{:S(2)}) collective-permute-start(bf16[512,256]{1,0:T(8,128)(2,1)} %refs_8_.3), channel_id=1, source_target_pairs={{0,16},{4,20},{8,24},{12,28},{16,0},{20,4},{24,8},{28,12},{1,17},{... | collective-permute-start | bytes 786440 | tf_op jit(solution)/shard_map/ppermute | solution.py:186
  1.2 8.8 %collective-permute-start.1 = (bf16[512,256]{1,0:T(8,128)(2,1)}, bf16[512,256]{1,0:T(8,128)(2,1)S(1)}, u32[]{:S(2)}, u32[]{:S(2)}) collective-permute-start(bf16[512,256]{1,0:T(8,128)(2,1)} %refs_0_.3), channel_id=1, source_target_pairs={{0,8},{4,12},{8,0},{12,4},{16,24},{20,28},{24,16},{28,20},{1,9},{5... | collective-permute-start | bytes 786440 | tf_op jit(solution)/shard_map/ppermute | solution.py:186
  1.5 11.5 %collective-permute-start.3 = (bf16[512,256]{1,0:T(8,128)(2,1)}, bf16[512,256]{1,0:T(8,128)(2,1)S(1)}, u32[]{:S(2)}, u32[]{:S(2)}) collective-permute-start(bf16[512,256]{1,0:T(8,128)(2,1)} %refs_0_.3), channel_id=1, source_target_pairs={{0,16},{4,20},{8,24},{12,28},{16,0},{20,4},{24,8},{28,12},{1,17},{... | collective-permute-start | bytes 786440 | tf_op jit(solution)/shard_map/ppermute | solution.py:186
  1.7 12.5 %collective-permute-start.8 = (bf16[512,256]{1,0:T(8,128)(2,1)}, bf16[512,256]{1,0:T(8,128)(2,1)S(1)}, u32[]{:S(2)}, u32[]{:S(2)}) collective-permute-start(bf16[512,256]{1,0:T(8,128)(2,1)} %refs_8_.3), channel_id=1, source_target_pairs={{0,8},{4,12},{8,0},{12,4},{16,24},{20,28},{24,16},{28,20},{1,9},{5... | collective-permute-start | bytes 786440 | tf_op jit(solution)/shard_map/ppermute | solution.py:186
  2.9 14.3 %collective-permute-start = (bf16[512,256]{1,0:T(8,128)(2,1)}, bf16[512,256]{1,0:T(8,128)(2,1)S(1)}, u32[]{:S(2)}, u32[]{:S(2)}) collective-permute-start(bf16[512,256]{1,0:T(8,128)(2,1)} %refs_0_.3), channel_id=1, source_target_pairs={{0,4},{4,0},{8,12},{12,8},{16,20},{20,16},{24,28},{28,24},{1,5},{5... | collective-permute-start | bytes 786440 | tf_op jit(solution)/shard_map/ppermute | solution.py:186
  7.4 9.9 %collective-permute-start.7 = (bf16[512,256]{1,0:T(8,128)(2,1)}, bf16[512,256]{1,0:T(8,128)(2,1)S(1)}, u32[]{:S(2)}, u32[]{:S(2)}) collective-permute-start(bf16[512,256]{1,0:T(8,128)(2,1)} %refs_8_.3), channel_id=1, source_target_pairs={{0,4},{4,0},{8,12},{12,8},{16,20},{20,16},{24,28},{28,24},{1,5},{5... | collective-permute-start | bytes 786440 | tf_op jit(solution)/shard_map/ppermute | solution.py:186
  10.1 9.5 %collective-permute-start.12 = (bf16[512,256]{1,0:T(8,128)(2,1)S(1)}, bf16[512,256]{1,0:T(8,128)(2,1)S(1)}, u32[]{:S(2)}, u32[]{:S(2)}) collective-permute-start(bf16[512,256]{1,0:T(8,128)(2,1)S(1)} %collective-permute-done.10.refs_12_), channel_id=1, source_target_pairs={{0,8},{4,12},{8,0},{12,4},{16,24},{20,28},{24,16},{28,20},{1,9},{5... | collective-permute-start | bytes 786440 | tf_op jit(solution)/shard_map/ppermute | solution.py:186
  13.0 8.4 %collective-permute-start.5 = (bf16[512,256]{1,0:T(8,128)(2,1)S(1)}, bf16[512,256]{1,0:T(8,128)(2,1)S(1)}, u32[]{:S(2)}, u32[]{:S(2)}) collective-permute-start(bf16[512,256]{1,0:T(8,128)(2,1)S(1)} %collective-permute-done.1.refs_2_), channel_id=1, source_target_pairs={{0,16},{4,20},{8,24},{12,28},{16,0},{20,4},{24,8},{28,12},{1,17},{... | collective-permute-start | bytes 786440 | tf_op jit(solution)/shard_map/ppermute | solution.py:186
  14.2 7.5 %collective-permute-start.11 = (bf16[512,256]{1,0:T(8,128)(2,1)S(1)}, bf16[512,256]{1,0:T(8,128)(2,1)S(1)}, u32[]{:S(2)}, u32[]{:S(2)}) collective-permute-start(bf16[512,256]{1,0:T(8,128)(2,1)S(1)} %collective-permute-done.10.refs_12_), channel_id=1, source_target_pairs={{0,4},{4,0},{8,12},{12,8},{16,20},{20,16},{24,28},{28,24},{1,5},{5... | collective-permute-start | bytes 786440 | tf_op jit(solution)/shard_map/ppermute | solution.py:186
  17.3 4.7 %collective-permute-start.2 = (bf16[512,256]{1,0:T(8,128)(2,1)S(1)}, bf16[512,256]{1,0:T(8,128)(2,1)S(1)}, u32[]{:S(2)}, u32[]{:S(2)}) collective-permute-start(bf16[512,256]{1,0:T(8,128)(2,1)S(1)} %collective-permute-done.1.refs_2_), channel_id=1, source_target_pairs={{0,4},{4,0},{8,12},{12,8},{16,20},{20,16},{24,28},{28,24},{1,5},{5... | collective-permute-start | bytes 786440 | tf_op jit(solution)/shard_map/ppermute | solution.py:186
  17.3 4.7 %collective-permute-start.4 = (bf16[512,256]{1,0:T(8,128)(2,1)S(1)}, bf16[512,256]{1,0:T(8,128)(2,1)S(1)}, u32[]{:S(2)}, u32[]{:S(2)}) collective-permute-start(bf16[512,256]{1,0:T(8,128)(2,1)S(1)} %collective-permute-done.3.refs_4_), channel_id=1, source_target_pairs={{0,4},{4,0},{8,12},{12,8},{16,20},{20,16},{24,28},{28,24},{1,5},{5... | collective-permute-start | bytes 786440 | tf_op jit(solution)/shard_map/ppermute | solution.py:186
  19.5 3.0 %collective-permute-start.9 = (bf16[512,256]{1,0:T(8,128)(2,1)S(1)}, bf16[512,256]{1,0:T(8,128)(2,1)S(1)}, u32[]{:S(2)}, u32[]{:S(2)}) collective-permute-start(bf16[512,256]{1,0:T(8,128)(2,1)S(1)} %collective-permute-done.8.refs_10_), channel_id=1, source_target_pairs={{0,4},{4,0},{8,12},{12,8},{16,20},{20,16},{24,28},{28,24},{1,5},{5... | collective-permute-start | bytes 786440 | tf_op jit(solution)/shard_map/ppermute | solution.py:186
  21.4 1.5 collective-permute-start.13
  21.7 1.7 collective-permute-start.6
  23.5 0.7 copy-start
  45.7 31.3 %collective-permute-start.14 = (bf16[256,2048]{1,0:T(8,128)(2,1)S(1)}, bf16[256,2048]{1,0:T(8,128)(2,1)S(1)}, u32[]{:S(2)}, u32[]{:S(2)}) collective-permute-start(bf16[256,2048]{1,0:T(8,128)(2,1)S(1)} %share.14.refs_0_), channel_id=1, source_target_pairs={{0,1},{3,2},{4,5},{7,6},{8,9},{11,10},{12,13},{15,14},{16,17},{19,... | collective-permute-start | bytes 3145736 | tf_op jit(solution)/shard_map/ppermute | solution.py:283
  47.1 52.4 %collective-permute-start.18 = (bf16[256,2048]{1,0:T(8,128)(2,1)S(1)}, bf16[256,2048]{1,0:T(8,128)(2,1)S(1)}, u32[]{:S(2)}, u32[]{:S(2)}) collective-permute-start(bf16[256,2048]{1,0:T(8,128)(2,1)S(1)} %share.15.refs_16_), channel_id=1, source_target_pairs={{0,1},{3,2},{4,5},{7,6},{8,9},{11,10},{12,13},{15,14},{16,17},{19,... | collective-permute-start | bytes 3145736 | tf_op jit(solution)/shard_map/ppermute | solution.py:283
  82.0 25.9 %collective-permute-start.17 = (bf16[256,2048]{1,0:T(8,128)(2,1)S(1)}, bf16[256,2048]{1,0:T(8,128)(2,1)S(1)}, u32[]{:S(2)}, u32[]{:S(2)}) collective-permute-start(bf16[256,2048]{1,0:T(8,128)(2,1)S(1)} %share.17.refs_0_), channel_id=1, source_target_pairs={{1,2},{2,1},{5,6},{6,5},{9,10},{10,9},{13,14},{14,13},{17,18},{18,... | collective-permute-start | bytes 3145736 | tf_op jit(solution)/shard_map/ppermute | solution.py:283
  83.9 38.0 %collective-permute-start.16 = (bf16[256,2048]{1,0:T(8,128)(2,1)S(1)}, bf16[256,2048]{1,0:T(8,128)(2,1)S(1)}, u32[]{:S(2)}, u32[]{:S(2)}) collective-permute-start(bf16[256,2048]{1,0:T(8,128)(2,1)S(1)} %share.16.refs_1_), channel_id=1, source_target_pairs={{0,1},{3,2},{4,5},{7,6},{8,9},{11,10},{12,13},{15,14},{16,17},{19,... | collective-permute-start | bytes 3145736 | tf_op jit(solution)/shard_map/ppermute | solution.py:283
  104.6 46.2 %collective-permute-start.19 = (bf16[256,2048]{1,0:T(8,128)(2,1)S(1)}, bf16[256,2048]{1,0:T(8,128)(2,1)S(1)}, u32[]{:S(2)}, u32[]{:S(2)}) collective-permute-start(bf16[256,2048]{1,0:T(8,128)(2,1)S(1)} %share.19.refs_0_), channel_id=1, source_target_pairs={{1,2},{2,1},{5,6},{6,5},{9,10},{10,9},{13,14},{14,13},{17,18},{18,... | collective-permute-start | bytes 3145736 | tf_op jit(solution)/shard_map/ppermute | solution.py:283
  106.5 37.9 %collective-permute-start.15 = (bf16[256,2048]{1,0:T(8,128)(2,1)S(1)}, bf16[256,2048]{1,0:T(8,128)(2,1)S(1)}, u32[]{:S(2)}, u32[]{:S(2)}) collective-permute-start(bf16[256,2048]{1,0:T(8,128)(2,1)S(1)} %share.18.refs_1_), channel_id=1, source_target_pairs={{0,1},{3,2},{4,5},{7,6},{8,9},{11,10},{12,13},{15,14},{16,17},{19,... | collective-permute-start | bytes 3145736 | tf_op jit(solution)/shard_map/ppermute | solution.py:283
  112.9 39.8 %collective-permute-start.20 = (bf16[256,2048]{1,0:T(8,128)(2,1)S(1)}, bf16[256,2048]{1,0:T(8,128)(2,1)S(1)}, u32[]{:S(2)}, u32[]{:S(2)}) collective-permute-start(bf16[256,2048]{1,0:T(8,128)(2,1)S(1)} %share.22.refs_1_), channel_id=1, source_target_pairs={{1,0},{2,3},{5,4},{6,7},{9,8},{10,11},{13,12},{14,15},{17,16},{18,... | collective-permute-start | bytes 3145736 | tf_op jit(solution)/shard_map/ppermute | solution.py:283
  127.0 30.7 %collective-permute-start.23 = (bf16[256,2048]{1,0:T(8,128)(2,1)S(1)}, bf16[256,2048]{1,0:T(8,128)(2,1)S(1)}, u32[]{:S(2)}, u32[]{:S(2)}) collective-permute-start(bf16[256,2048]{1,0:T(8,128)(2,1)S(1)} %share.23.refs_0_), channel_id=1, source_target_pairs={{1,2},{2,1},{5,6},{6,5},{9,10},{10,9},{13,14},{14,13},{17,18},{18,... | collective-permute-start | bytes 3145736 | tf_op jit(solution)/shard_map/ppermute | solution.py:283
  128.9 38.0 %collective-permute-start.25 = (bf16[256,2048]{1,0:T(8,128)(2,1)S(1)}, bf16[256,2048]{1,0:T(8,128)(2,1)S(1)}, u32[]{:S(2)}, u32[]{:S(2)}) collective-permute-start(bf16[256,2048]{1,0:T(8,128)(2,1)S(1)} %share.20.refs_0_), channel_id=1, source_target_pairs={{0,1},{3,2},{4,5},{7,6},{8,9},{11,10},{12,13},{15,14},{16,17},{19,... | collective-permute-start | bytes 3145736 | tf_op jit(solution)/shard_map/ppermute | solution.py:283
  144.4 34.0 %collective-permute-start.22 = (bf16[256,2048]{1,0:T(8,128)(2,1)S(1)}, bf16[256,2048]{1,0:T(8,128)(2,1)S(1)}, u32[]{:S(2)}, u32[]{:S(2)}) collective-permute-start(bf16[256,2048]{1,0:T(8,128)(2,1)S(1)} %share.21.refs_1_), channel_id=1, source_target_pairs={{0,1},{3,2},{4,5},{7,6},{8,9},{11,10},{12,13},{15,14},{16,17},{19,... | collective-permute-start | bytes 3145736 | tf_op jit(solution)/shard_map/ppermute | solution.py:283
  150.7 27.7 %collective-permute-start.21 = (bf16[256,2048]{1,0:T(8,128)(2,1)S(1)}, bf16[256,2048]{1,0:T(8,128)(2,1)S(1)}, u32[]{:S(2)}, u32[]{:S(2)}) collective-permute-start(bf16[256,2048]{1,0:T(8,128)(2,1)S(1)} %share.25.refs_0_), channel_id=1, source_target_pairs={{1,2},{2,1},{5,6},{6,5},{9,10},{10,9},{13,14},{14,13},{17,18},{18,... | collective-permute-start | bytes 3145736 | tf_op jit(solution)/shard_map/ppermute | solution.py:283
  157.7 9.2 %copy-start.1 = (s32[16]{0:T(128)S(1)}, s32[16]{0:T(128)}, u32[]{:S(2)}) copy-start(s32[16]{0:T(128)} %order_ref.7) | copy-start | bytes 196
  162.7 15.7 %collective-permute-start.24 = (bf16[256,2048]{1,0:T(8,128)(2,1)S(1)}, bf16[256,2048]{1,0:T(8,128)(2,1)S(1)}, u32[]{:S(2)}, u32[]{:S(2)}) collective-permute-start(bf16[256,2048]{1,0:T(8,128)(2,1)S(1)} %share.27), channel_id=1, source_target_pairs={{1,0},{2,3},{5,4},{6,7},{9,8},{10,11},{13,12},{14,15},{17,16},{18,... | collective-permute-start | bytes 3145736 | tf_op jit(solution)/shard_map/ppermute | solution.py:283
